TPU v7x, 256 devices: a whole 4x4x8 slice. The times are simulated.
256 devices in a mesh: ctx: 64 (over y, z, core), head: 4 (over x).
Axes of the slice: x: 4, y: 4, z: 8, core: 2. Of those that a mesh axis runs over, the one named last changes fastest.
Arguments:
- queries: bfloat16 [32768, 512], P('ctx', 'head'), may hold values from -400 to 400
- keys: bfloat16 [32768, 128], P('ctx'), may hold values from -4 to 4
- values: bfloat16 [32768, 128], P('ctx'), may hold values from -6 to 6
Outputs:
- attended: bfloat16 [32768, 512], P('ctx', 'head')
All inputs are finite; a program needn't handle non-finite values.
Results may differ from a plain program's by a relative error of at most 0.0065.
Values may be sent and summed in bfloat16 or wider, within the bound.
A program may use at most 64 MiB of HBM per device.

v0:
```python
import math

import jax
import jax.numpy as jnp
from jax import lax
from jax.sharding import PartitionSpec as P


def empty_state(query_count, head_size):
    return (
        jnp.full((query_count,), -1e30, jnp.float32),
        jnp.zeros((query_count,), jnp.float32),
        jnp.zeros((query_count, head_size), jnp.float32),
    )


def attend_block(state_one, query_set, key_block, value_block, block_offset, score_scale):
    query_rows, query_pos, key_low, key_high, query_top = query_set
    running_max, running_sum, accumulated = state_one
    row_count = key_block.shape[0]

    def update(unused):
        scores = (
            jnp.einsum("qd,kd->qk", query_rows, key_block, preferred_element_type=jnp.float32)
            * score_scale
        )
        key_pos = block_offset + jnp.arange(row_count, dtype=jnp.int32)
        visible = (
            (key_pos[None, :] <= query_pos[:, None])
            & (key_pos >= key_low)[None, :]
            & (key_pos < key_high)[None, :]
        )
        block_max = jnp.max(jnp.where(visible, scores, -1e30), axis=1)
        new_max = jnp.maximum(running_max, block_max)
        weights = jnp.where(visible, jnp.exp(scores - new_max[:, None]), 0.0)
        rescale = jnp.exp(running_max - new_max)
        new_sum = running_sum * rescale + jnp.sum(weights, axis=1)
        product = jnp.dot(
            weights.astype(jnp.bfloat16), value_block, preferred_element_type=jnp.float32
        )
        return (new_max, new_sum, accumulated * rescale[:, None] + product)

    def keep(unused):
        return state_one

    needed = (
        (block_offset < key_high)
        & (block_offset + row_count > key_low)
        & (block_offset <= query_top)
    )
    return lax.cond(needed, update, keep, 0)


def fold_keys(query_sets, score_scale):

    def folded(carried, pieces, offset):
        key_piece, value_piece = pieces
        total_rows = key_piece.shape[0]
        block_rows = 512
        block_count = total_rows // block_rows
        key_blocks = key_piece.reshape(block_count, block_rows, key_piece.shape[1])
        value_blocks = value_piece.reshape(block_count, block_rows, value_piece.shape[1])
        offsets = jnp.arange(block_count, dtype=jnp.int32) * block_rows

        def across(states, blocks):
            key_block, value_block, block_offset = blocks
            updated = tuple(
                (
                    attend_block(
                        state_one, query_set, key_block, value_block, block_offset, score_scale
                    )
                    for state_one, query_set in zip(states, query_sets)
                )
            )
            return (updated, None)

        result, unused = lax.scan(across, carried, (key_blocks, value_blocks, offsets))
        return result

    return folded


def body(queries, keys, values):
    query_count = queries.shape[0]
    head_size = keys.shape[1]
    score_scale = 1.0 / math.sqrt(head_size)
    position = lax.axis_index("ctx")
    own_start = position * query_count
    row_steps = jnp.arange(query_count, dtype=jnp.int32)
    query_sets = (
        (queries, own_start + row_steps, 0, own_start + query_count, own_start + query_count - 1),
    )
    initial = tuple((empty_state(query_count, head_size) for entry in query_sets))
    folded = fold_keys(query_sets, score_scale)
    states = folded(
        initial,
        (
            lax.all_gather(keys, "ctx", axis=0, tiled=True),
            lax.all_gather(values, "ctx", axis=0, tiled=True),
        ),
        jnp.int32(0),
    )
    own_max, own_sum, own_acc = states[0]
    return (own_acc / own_sum[:, None]).astype(jnp.bfloat16)


def solution(mesh):
    placed = (P("ctx", "head"), P("ctx", None), P("ctx", None))
    return jax.shard_map(
        body, mesh=mesh, in_specs=placed, out_specs=P("ctx", "head"), check_vma=False
    )
```

profile of v0, /device:TPU:255, one launch (start us, length us, event | category | flops | bytes accessed | tf_op | source)
XLA Modules:
  0.0 649.1 jit_solution(17132130347548404904)
XLA Ops:
  8.0 83.0 %all-gather.3.cloned.1.call-done = bf16[32768,128]{1,0:T(8,128)(2,1)} async-done(((bf16[512,128]{1,0:T(8,128)(2,1)}), bf16[32768,128]{1,0:T(8,128)(2,1)}) %all-gather.3.cloned.1.call-update) | async-done | bytes 8388624 | tf_op jit(solution)/shard_map/all_gather | solution.py:98
  91.0 83.1 %all-gather.5.cloned.1.call-done = bf16[32768,128]{1,0:T(8,128)(2,1)} async-done(((bf16[512,128]{1,0:T(8,128)(2,1)}), bf16[32768,128]{1,0:T(8,128)(2,1)}) %all-gather.5.cloned.1.call-update) | async-done | bytes 8388624 | tf_op jit(solution)/shard_map/all_gather | solution.py:99
  174.2 467.3 %while.15 = (s32[]{:T(128)}, f32[512]{0:T(512)S(1)}, f32[512]{0:T(512)S(1)}, f32[512,128]{1,0:T(8,128)S(1)}, s32[64]{0:T(128)S(1)}, /*index=5*/s32[]{:T(128)}, s...) while((s32[]{:T(128)}, f32[512]{0:T(512)S(1)}, ...), condition=%wide.region_5.6_spmd.clone, body=%wide.region_0.5_spmd.clone.sunk | while | flops 139070976 | bytes 4121955 | solution.py:77
  176.7 4.7 conditional.3
  184.0 4.7 conditional.3
  198.6 4.7 conditional.3
  205.9 4.7 conditional.3
  220.5 4.7 conditional.3
  235.1 4.7 conditional.3
  242.4 4.7 conditional.3
  257.0 4.7 conditional.3
  264.3 4.7 conditional.3
  278.9 4.7 conditional.3
  286.2 4.7 conditional.3
  300.8 4.7 conditional.3
  315.4 4.7 conditional.3
  322.7 4.7 conditional.3
  337.3 4.7 conditional.3
  344.6 4.7 conditional.3
  359.2 4.7 conditional.3
  373.8 4.7 conditional.3
  381.1 4.7 conditional.3
  395.7 4.7 conditional.3
  403.0 4.7 conditional.3
  (692 shorter events, 545.1 us)
Async XLA Ops:
  6.5 84.5 %all-gather.3.cloned.1.call-start = ((), (), s32[]{:S(2)}) async-start(), calls=%async_computation | async-start | bytes 8519680 | tf_op jit(solution)/shard_map/all_gather | solution.py:98
  7.3 166.9 %all-gather.5.cloned.1.call-start = ((), (), s32[]{:S(2)}) async-start(), calls=%async_computation.1 | async-start | bytes 8519680 | tf_op jit(solution)/shard_map/all_gather | solution.py:99
Sparse Core Ops, SparseCore 0:
  10.1 80.8 all-gather.2
  93.8 80.2 all-gather.4
where the time goes:
time: 654 us; the launch traced here: 649 us
  matrix products  191 us (29%)
  waiting for transfers between devices  168 us (26%)
  loops' own time  128 us (20%)
  other arithmetic  109 us (17%)
  local copies, waits for them, and re-layouts  39.3 us (6%)
  between operations  13.4 us (2%)
    another operation x1, loops' own time, folded(): lax.scan(across, carried, (key_blocks, value_blocks, offsets))  125 us
    dot_general x64, matrix products, update(): jnp.dot(weights.astype(jnp.bfloat16), value_block, preferred_element_type...  101 us
    dot_general x64, matrix products, update(): jnp.einsum('qd,kd->qk', query_rows, key_block, preferred_element_type=jnp...  90.1 us
    all_gather x1, waiting for transfers between devices, body(): lax.all_gather(values, 'ctx', axis=0, tiled=True)  83.1 us
    all_gather x1, waiting for transfers between devices, body(): lax.all_gather(keys, 'ctx', axis=0, tiled=True)  83 us
    lt x64, other arithmetic, update(): key_pos < key_high  40.9 us
    add x64, other arithmetic, update(): key_pos = block_offset + jnp.arange(row_count, dtype=jnp.int32)  40.7 us
    dynamic_slice x64, local copies, waits for them, and re-layouts, folded(): lax.scan(across, carried, (key_blocks, value_blocks, offsets))  39 us
  transfers between devices with their start and end apart: 2, of which 2 were waited for; matrix products, arithmetic and copies ran while one was open for 0% of the time, Pallas kernels for 0%

commit v1 on v0

v1 whole, which is shorter than its diff:
```python
import math

import jax
import jax.numpy as jnp
from jax import lax
from jax.experimental import pallas as pl
from jax.experimental.pallas import tpu as pltpu
from jax.sharding import PartitionSpec as P

MESH = pl.DeviceIdType.MESH
NX, NY, NZ = 4, 4, 8
BLK = 128
HD = 128
COLS = NX * BLK
SCALE = math.log2(math.e) / math.sqrt(HD)
EMPTY = -1e30
HIDDEN = -2e30
ORDER = (2, 3, 0, 1)
F32 = jnp.float32
BF16 = jnp.bfloat16


def kernel(
    q_ref, k_ref, v_ref, o_ref,
    kv, qown, qb, s0, s1, s2, s3, mx, mp, ls, acc, osend, orecv,
    rs, zs, ys, yo, ss, sr, qss, qrs, oss, ors,
):
    scores = (s0, s1, s2, s3)
    ctx, x = lax.axis_index("ctx"), lax.axis_index("head")
    c = lax.rem(ctx, 2)
    z = lax.rem(lax.div(ctx, 2), NZ)
    y = lax.div(ctx, 2 * NZ)
    opp = lax.rem(y + 2, NY)
    yup, ydn = lax.rem(y + 1, NY), lax.rem(y + NY - 1, NY)
    zup, zdn = lax.rem(z + 1, NZ), lax.rem(z + NZ - 1, NZ)
    peers = [(dx, dy) for dy in range(NY) for dx in range(NX) if dx or dy]

    def dev(xx, yy, zz, cc):
        return ((yy * NZ + zz) * 2 + cc, xx)

    def copy(src, dst, send, recv, device):
        return pltpu.make_async_remote_copy(
            src_ref=src, dst_ref=dst, send_sem=send, recv_sem=recv, device_id=device, device_id_type=MESH
        )

    barrier = pltpu.get_barrier_semaphore()
    targets = [dev(lax.rem(x + dx, NX), lax.rem(y + dy, NY), z, c) for dx, dy in peers]
    targets += [dev(x, y, zup, c), dev(x, y, zdn, c), dev(x, y, z, 1 - c)]
    for target in targets:
        pl.semaphore_signal(barrier, inc=1, device_id=target, device_id_type=MESH)

    def turn(a):
        return a.astype(F32).T.astype(BF16)

    rows = pl.ds(pl.multiple_of(x * BLK, BLK), BLK)
    for r in range(NY):
        qown[r] = turn(q_ref[r * BLK:(r + 1) * BLK, :])
    qb[y, x] = qown[y]
    kv[z, c, y, :BLK, :] = k_ref[rows, :]
    kv[z, c, y, BLK:, :] = turn(v_ref[rows, :])
    for g in range(NY):
        mx[g] = jnp.full((1, COLS), EMPTY, F32)
        ls[g] = jnp.zeros((1, COLS), F32)
        acc[g] = jnp.zeros((HD, COLS), F32)

    pl.semaphore_wait(barrier, len(targets))

    def q_copy(dx, dy):
        yy = lax.rem(y + dy, NY)
        i = dy * NX + dx
        return copy(qown.at[yy], qb.at[y, x], qss.at[i], qrs.at[i], dev(lax.rem(x + dx, NX), yy, z, c))

    def kv_send(zz, yy, send, device):
        part = kv.at[zz, c, yy]
        copy(part, part, send, rs.at[zz, yy], device).start()

    def kv_wait(zz, yy):
        part = kv.at[zz, c, yy]
        copy(part, part, yo.at[0], rs.at[zz, yy], dev(x, y, z, 1 - c)).wait_recv()

    kv_send(z, y, yo.at[0], dev(x, opp, z, c))
    for dx, dy in peers:
        q_copy(dx, dy).start()
    kv_send(z, y, zs.at[0, 0], dev(x, y, zdn, c))
    kv_send(z, y, zs.at[0, 7], dev(x, y, zup, c))
    kv_send(z, y, ys.at[0, 0], dev(x, yup, z, c))
    kv_send(z, y, ys.at[1, 0], dev(x, ydn, z, c))

    def place(n):
        d = lax.div(n + 1, 2)
        return lax.rem(z + NZ + d * (2 * lax.rem(n, 2) - 1), NZ)

    def stage_z(n):
        zz = place(n)
        odd = lax.rem(n, 2)
        nxt = odd * zdn + (1 - odd) * zup
        kv_wait(zz, y)

        @pl.when((n <= 4) | (n == 6))
        def _():
            kv_send(zz, y, zs.at[0, n], dev(x, y, nxt, c))

        kv_send(zz, y, ys.at[0, n], dev(x, yup, z, c))
        kv_send(zz, y, ys.at[1, n], dev(x, ydn, z, c))
        kv_wait(zz, opp)

        @pl.when(n <= 5)
        def _():
            kv_send(zz, opp, zs.at[1, n], dev(x, y, nxt, c))

    def both_copy(n):
        zz = place(n)
        part = kv.at[zz, c]
        return copy(part, part, ss.at[n], sr.at[zz], dev(x, y, z, 1 - c))

    def stage_y(n):
        zz = place(n)
        kv_wait(zz, yup)
        kv_wait(zz, ydn)
        both_copy(n).start()

    def stage_c(n):
        zz = place(n)
        part = kv.at[zz, 1 - c]
        copy(part, part, ss.at[0], sr.at[zz], dev(x, y, z, 1 - c)).wait_recv()

    kv_wait(z, opp)
    kv_send(z, opp, zs.at[1, 0], dev(x, y, zdn, c))
    kv_send(z, opp, zs.at[1, 7], dev(x, y, zup, c))
    stage_y(jnp.int32(0))
    stage_z(jnp.int32(1))
    stage_z(jnp.int32(2))
    stage_y(jnp.int32(1))
    for dx, dy in peers:
        q_copy(dx, dy).wait_recv()
    stage_c(jnp.int32(0))

    apart = lax.broadcasted_iota(jnp.int32, (BLK, COLS), 0) - lax.rem(
        lax.broadcasted_iota(jnp.int32, (BLK, COLS), 1), BLK
    )

    def score(n, g):
        zz = place(n)
        depth = (g + 1) * BLK
        k = kv[zz, :, :g + 1, :BLK, :].reshape(2 * depth, HD)
        q = jnp.concatenate([qb[g, h] for h in range(NX)], axis=1)
        s = jnp.dot(k, q, preferred_element_type=F32)
        parts = []
        for cc in range(2):
            ahead = (zz - z) * 1024 + (cc - c) * 512 + (x - y) * BLK
            last = s[(cc + 1) * depth - BLK:(cc + 1) * depth]
            parts.append(s[cc * depth:(cc + 1) * depth - BLK])
            parts.append(jnp.where(apart <= -ahead, last, HIDDEN))
        s = jnp.concatenate([p for p in parts if p.shape[0]], axis=0)
        scores[g][...] = s
        before = mx[g]
        mp[g] = before
        mx[g] = jnp.maximum(before, jnp.max(s, axis=0, keepdims=True))

    def weigh(n, g, before, now):
        zz = place(n)
        p = jnp.exp2(scores[g][...] * SCALE - now * SCALE)
        v = jnp.concatenate([kv[zz, cc, yy, BLK:, :] for cc in range(2) for yy in range(g + 1)], axis=1)
        old = jnp.exp2((before - now) * SCALE)
        ls[g] = ls[g] * old + jnp.sum(p, axis=0, keepdims=True)
        acc[g] = acc[g] * old + jnp.dot(v, p.astype(BF16), preferred_element_type=F32)

    def step(n, g, m, g_next):
        before, now = mp[g], mx[g]
        score(m, g_next)
        weigh(n, g, before, now)

    score(jnp.int32(0), ORDER[0])

    def unit(n, carry):
        for i in range(NY - 1):
            step(n, ORDER[i], n, ORDER[i + 1])

        @pl.when(n + 3 < NZ)
        def _():
            stage_z(n + 3)

        @pl.when(n + 2 < NZ)
        def _():
            stage_y(n + 2)

        @pl.when(n + 1 < NZ)
        def _():
            stage_c(n + 1)

        step(n, ORDER[NY - 1], jnp.minimum(n + 1, NZ - 1), ORDER[0])
        return carry

    lax.fori_loop(0, NZ, unit, 0)

    line = lax.broadcasted_iota(jnp.int32, (16, BLK), 0)

    def thirds(a):
        high = a.astype(BF16).astype(F32)
        mid = (a - high).astype(BF16).astype(F32)
        return high, mid, a - high - mid

    def finish(g):
        total = acc[g].astype(BF16)
        for h in range(NX):
            lanes = slice(h * BLK, (h + 1) * BLK)
            osend[g, h, :HD, :] = total[:, lanes]
            now, count = mx[g][:, lanes], ls[g][:, lanes]
            side = jnp.zeros((16, BLK), F32)
            for i, part in enumerate(thirds(now) + thirds(count)):
                side = jnp.where(line == i, part, side)
            osend[g, h, HD:, :] = side.astype(BF16)

    def o_copy(dx, dy):
        xx, yy = lax.rem(x + dx, NX), lax.rem(y + dy, NY)
        i = dy * NX + dx
        return copy(osend.at[yy, xx], orecv.at[y, x], oss.at[i], ors.at[i], dev(xx, yy, z, c))

    for g in range(NY):
        finish(g)
    for dx, dy in peers:
        o_copy(dx, dy).start()
    orecv[y, x] = osend[y, x]

    here = dev(x, y, z, 1 - c)
    one = kv.at[z, c, y]
    for n in range(NZ):
        if n != 5:
            copy(one, one, zs.at[0, n], rs.at[z, y], here).wait_send()
        if n != 6:
            copy(one, one, zs.at[1, n], rs.at[z, y], here).wait_send()
        for way in range(2):
            copy(one, one, ys.at[way, n], rs.at[z, y], here).wait_send()
        both_copy(jnp.int32(n)).wait_send()
    copy(one, one, yo.at[0], rs.at[z, y], here).wait_send()
    for dx, dy in peers:
        q_copy(dx, dy).wait_send()

    for dx, dy in peers:
        o_copy(dx, dy).wait_recv()

    def combine(r):
        sides = [orecv[r, h, HD:, :].astype(F32) for h in range(NX)]
        tops = [side[0:1] + side[1:2] + side[2:3] for side in sides]
        counts = [side[3:4] + side[4:5] + side[5:6] for side in sides]
        top = jnp.maximum(jnp.maximum(tops[0], tops[1]), jnp.maximum(tops[2], tops[3]))
        shares = [jnp.exp2((t - top) * SCALE) for t in tops]
        inverse = 1.0 / sum(share * count for share, count in zip(shares, counts))
        total = sum((share * inverse) * orecv[r, h, :HD, :].astype(F32) for h, share in enumerate(shares))
        o_ref[r * BLK:(r + 1) * BLK, :] = total.T.astype(BF16)

    for r in range(NY):
        combine(r)
    for dx, dy in peers:
        o_copy(dx, dy).wait_send()


def body(queries, keys, values):
    vmem = pl.BlockSpec(memory_space=pltpu.VMEM)
    dma = pltpu.SemaphoreType.DMA
    scratch = [
        pltpu.VMEM((NZ, 2, NY, 2 * BLK, HD), BF16),
        pltpu.VMEM((NY, HD, BLK), BF16),
        pltpu.VMEM((NY, NX, HD, BLK), BF16),
    ]
    scratch += [pltpu.VMEM((2 * BLK * (g + 1), COLS), F32) for g in range(NY)]
    scratch += [pltpu.VMEM((NY, 1, COLS), F32) for _ in range(3)]
    scratch += [
        pltpu.VMEM((NY, HD, COLS), F32),
        pltpu.VMEM((NY, NX, HD + 16, BLK), BF16),
        pltpu.VMEM((NY, NX, HD + 16, BLK), BF16),
        dma((NZ, NY)), dma((2, NZ)), dma((2, NZ)), dma((1,)), dma((NZ,)), dma((NZ,)),
        dma((16,)), dma((16,)), dma((16,)), dma((16,)),
    ]
    return pl.pallas_call(
        kernel,
        out_shape=jax.ShapeDtypeStruct(queries.shape, BF16),
        in_specs=[vmem] * 3,
        out_specs=vmem,
        scratch_shapes=scratch,
        compiler_params=pltpu.CompilerParams(
            collective_id=0, has_side_effects=True, vmem_limit_bytes=40 * 1024 * 1024
        ),
    )(queries, keys, values)


def solution(mesh):
    placed = (P("ctx", "head"), P("ctx", None), P("ctx", None))
    return jax.shard_map(
        body, mesh=mesh, in_specs=placed, out_specs=P("ctx", "head"), check_vma=False
    )
```

time: 654 us -> 60.3 us (0.09)
  the two profiles are of different devices: /device:TPU:255 before, /device:TPU:1 now
where the time goes in v1:
time: 60.3 us; the launch traced here: 59.3 us
  Pallas kernels  56 us (93%)
  local copies, waits for them, and re-layouts  3.37 us (6%)
    pallas_call x1, Pallas kernels, body(): pl.pallas_call(kernel, out_shape=jax.ShapeDtypeStruct(queries.shape, BF16...  56 us
    unnamed x7, local copies, waits for them, and re-layouts  3.37 us

profile of v1, /device:TPU:1, one launch (start us, length us, event | category | flops | bytes accessed | tf_op | source)
XLA Modules:
  0.0 59.3 jit_solution(7881715806653108993)
XLA Ops:
  0.0 0.0 copy-start
  0.0 0.9 %copy-done = bf16[512,128]{1,0:T(8,128)(2,1)S(1)} copy-done((bf16[512,128]{1,0:T(8,128)(2,1)S(1)}, bf16[512,128]{1,0:T(8,128)(2,1)}, u32[]{:S(2)}) %copy-start) | copy-done | bytes 131096
  0.9 0.0 copy-start.1
  0.9 0.9 %copy-done.1 = bf16[512,128]{1,0:T(8,128)(2,1)S(1)} copy-done((bf16[512,128]{1,0:T(8,128)(2,1)S(1)}, bf16[512,128]{1,0:T(8,128)(2,1)}, u32[]{:S(2)}) %copy-start.1) | copy-done | bytes 131096
  1.8 0.0 copy-start.2
  1.8 0.9 %copy-done.2 = bf16[512,128]{1,0:T(8,128)(2,1)S(1)} copy-done((bf16[512,128]{1,0:T(8,128)(2,1)S(1)}, bf16[512,128]{1,0:T(8,128)(2,1)}, u32[]{:S(2)}) %copy-start.2) | copy-done | bytes 131096
  2.7 56.0 %shard_map.37 = bf16[512,128]{1,0:T(8,128)(2,1)S(1)} custom-call(bf16[512,128]{1,0:T(8,128)(2,1)S(1)} %copy-done, bf16[512,128]{1,0:T(8,128)(2,1)S(1)} %copy-done.1, bf16[512,128]{1,0:T(8,128)(2,1)S(1)} %copy-done.2), custom_call_target="tpu_custom_call" | custom-call | tf_op jit(solution)/shard_map/pallas_call | solution.py:275
  58.7 0.7 %copy.5 = bf16[512,128]{1,0:T(8,128)(2,1)} copy(bf16[512,128]{1,0:T(8,128)(2,1)S(1)} %shard_map.37) | data formatting | bytes 262144
Async XLA Ops:
  0.0 0.9 %copy-start = (bf16[512,128]{1,0:T(8,128)(2,1)S(1)}, bf16[512,128]{1,0:T(8,128)(2,1)}, u32[]{:S(2)}) copy-start(bf16[512,128]{1,0:T(8,128)(2,1)} %q_ref.1) | copy-start | bytes 393220
  0.9 0.9 %copy-start.1 = (bf16[512,128]{1,0:T(8,128)(2,1)S(1)}, bf16[512,128]{1,0:T(8,128)(2,1)}, u32[]{:S(2)}) copy-start(bf16[512,128]{1,0:T(8,128)(2,1)} %k_ref.1) | copy-start | bytes 393220
  1.8 0.9 %copy-start.2 = (bf16[512,128]{1,0:T(8,128)(2,1)S(1)}, bf16[512,128]{1,0:T(8,128)(2,1)}, u32[]{:S(2)}) copy-start(bf16[512,128]{1,0:T(8,128)(2,1)} %v_ref.1) | copy-start | bytes 393220

commit v2 on v1

v2 whole, which is shorter than its diff:
```python
import math

import jax
import jax.numpy as jnp
from jax import lax
from jax.experimental import pallas as pl
from jax.experimental.pallas import tpu as pltpu
from jax.sharding import PartitionSpec as P

MESH = pl.DeviceIdType.MESH
NX, NY, NZ = 4, 4, 8
BLK = 128
HD = 128
COLS = 512
SCALE = math.log2(math.e) / math.sqrt(HD)
EMPTY = -1e30
HIDDEN = -2e30
WAYS = (2, 1, 3)
F32 = jnp.float32
BF16 = jnp.bfloat16


def kernel(
    q_hbm, k_hbm, v_hbm, o_ref,
    q_ref, k_ref, v_ref, kv, qb, s0, s1, s2, s3, mx, mp, ls, acc, osend, orecv,
    ins, rs, zs, ys, yo, ss, sr, qss, qrs, oss, ors,
):
    scores = (s0, s1, s2, s3)
    ctx, x = lax.axis_index("ctx"), lax.axis_index("head")
    c = lax.rem(ctx, 2)
    z = lax.rem(lax.div(ctx, 2), NZ)
    y = lax.div(ctx, 2 * NZ)
    opp = lax.rem(y + 2, NY)
    yup, ydn = lax.rem(y + 1, NY), lax.rem(y + NY - 1, NY)
    zup, zdn = lax.rem(z + 1, NZ), lax.rem(z + NZ - 1, NZ)

    def dev(xx, yy, zz, cc):
        return ((yy * NZ + zz) * 2 + cc, xx)

    def copy(src, dst, send, recv, device):
        return pltpu.make_async_remote_copy(
            src_ref=src, dst_ref=dst, send_sem=send, recv_sem=recv, device_id=device, device_id_type=MESH
        )

    rows = pl.ds(pl.multiple_of(x * BLK, BLK), BLK)
    loads = [
        pltpu.make_async_copy(q_hbm, q_ref, ins.at[0]),
        pltpu.make_async_copy(k_hbm.at[rows], k_ref, ins.at[1]),
        pltpu.make_async_copy(v_hbm.at[rows], v_ref, ins.at[2]),
    ]
    for load in loads:
        load.start()
    barrier = pltpu.get_barrier_semaphore()
    targets = [dev(lax.rem(x + dx, NX), y, z, c) for dx in WAYS]
    targets += [dev(x, yy, z, c) for yy in (opp, yup, ydn)]
    targets += [dev(x, y, zup, c), dev(x, y, zdn, c), dev(x, y, z, 1 - c)]
    for target in targets:
        pl.semaphore_signal(barrier, inc=1, device_id=target, device_id_type=MESH)

    def turn(a):
        return a.astype(F32).T.astype(BF16)

    for g in range(NY):
        mx[g] = jnp.full((1, COLS), EMPTY, F32)
        ls[g] = jnp.zeros((1, COLS), F32)
        acc[g] = jnp.zeros((HD, COLS), F32)
    loads[0].wait()
    qb[x] = turn(q_ref[...])
    loads[1].wait()
    kv[z, c, y, :BLK, :] = k_ref[...]
    loads[2].wait()
    kv[z, c, y, BLK:, :] = turn(v_ref[...])

    pl.semaphore_wait(barrier, len(targets))

    def q_copy(dx):
        part = qb.at[x]
        return copy(part, part, qss.at[dx], qrs.at[dx], dev(lax.rem(x + dx, NX), y, z, c))

    def kv_send(zz, yy, send, device):
        part = kv.at[zz, c, yy]
        copy(part, part, send, rs.at[zz, yy], device).start()

    def kv_wait(zz, yy):
        part = kv.at[zz, c, yy]
        copy(part, part, yo.at[0], rs.at[zz, yy], dev(x, y, z, 1 - c)).wait_recv()

    kv_send(z, y, yo.at[0], dev(x, opp, z, c))
    kv_send(z, y, zs.at[0, 0], dev(x, y, zdn, c))
    kv_send(z, y, zs.at[0, 7], dev(x, y, zup, c))
    kv_send(z, y, ys.at[0, 0], dev(x, yup, z, c))
    kv_send(z, y, ys.at[1, 0], dev(x, ydn, z, c))
    for dx in (1, 3, 2):
        q_copy(dx).start()

    def place(n):
        d = lax.div(n + 1, 2) if not isinstance(n, int) else (n + 1) // 2
        side = 2 * (n % 2 if isinstance(n, int) else lax.rem(n, 2)) - 1
        return lax.rem(z + NZ + d * side, NZ)

    def onward(n):
        odd = n % 2 if isinstance(n, int) else lax.rem(n, 2)
        return dev(x, y, odd * zdn + (1 - odd) * zup, c)

    def stage_own(n):
        zz = place(n)
        kv_wait(zz, y)
        if n in (1, 2, 3, 4, 6):
            kv_send(zz, y, zs.at[0, n], onward(n))
        kv_send(zz, y, ys.at[0, n], dev(x, yup, z, c))
        kv_send(zz, y, ys.at[1, n], dev(x, ydn, z, c))

    def stage_opp(n):
        zz = place(n)
        kv_wait(zz, opp)
        if isinstance(n, int):
            if n <= 5:
                kv_send(zz, opp, zs.at[1, n], onward(n))
        else:

            @pl.when(n <= 5)
            def _():
                kv_send(zz, opp, zs.at[1, n], onward(n))

    def both_copy(n):
        zz = place(n)
        part = kv.at[zz, c]
        return copy(part, part, ss.at[n], sr.at[zz], dev(x, y, z, 1 - c))

    def stage_y(n):
        zz = place(n)
        kv_wait(zz, yup)
        kv_wait(zz, ydn)
        both_copy(n).start()

    def stage_c(n):
        zz = place(n)
        part = kv.at[zz, 1 - c]
        copy(part, part, ss.at[0], sr.at[zz], dev(x, y, z, 1 - c)).wait_recv()

    stage_own(1)
    stage_own(2)
    kv_wait(z, opp)
    kv_send(z, opp, zs.at[1, 0], dev(x, y, zdn, c))
    kv_send(z, opp, zs.at[1, 7], dev(x, y, zup, c))
    stage_y(0)
    stage_own(3)
    stage_own(4)
    stage_c(0)

    apart = lax.broadcasted_iota(jnp.int32, (BLK, COLS), 0) - lax.broadcasted_iota(jnp.int32, (BLK, COLS), 1)

    def slab(back):
        return lax.rem(y + NY - back, NY)

    def score(n, dx, to):
        zz, h = place(n), lax.rem(x + dx, NX)
        k = jnp.concatenate([kv[zz, :, slab(back), :BLK, :].reshape(2 * BLK, HD) for back in range(NY)], axis=0)
        s = jnp.dot(k, qb[h], preferred_element_type=F32)
        parts = []
        for cc in range(2):
            ahead = (zz - z) * 1024 + (cc - c) * 512 + x * BLK
            parts.append(jnp.where(apart <= -ahead, s[cc * BLK:(cc + 1) * BLK], HIDDEN))
        for back in range(1, NY):
            parts.append(jnp.where(back <= y, s[2 * back * BLK:2 * (back + 1) * BLK], HIDDEN))
        s = jnp.concatenate(parts, axis=0)
        to[...] = s
        before = mx[dx]
        mp[dx] = before
        mx[dx] = jnp.maximum(before, jnp.max(s, axis=0, keepdims=True))

    def weigh(n, dx, at, before, now):
        zz = place(n)
        old = jnp.exp2((before - now) * SCALE)
        p = jnp.exp2(at[...] * SCALE - now * SCALE)
        v = jnp.concatenate([kv[zz, cc, slab(back), BLK:, :] for back in range(NY) for cc in range(2)], axis=1)
        ls[dx] = ls[dx] * old + jnp.sum(p, axis=0, keepdims=True)
        acc[dx] = acc[dx] * old + jnp.dot(v, p.astype(BF16), preferred_element_type=F32)

    line = lax.broadcasted_iota(jnp.int32, (16, COLS), 0)

    def thirds(a):
        high = a.astype(BF16).astype(F32)
        mid = (a - high).astype(BF16).astype(F32)
        return high, mid, a - high - mid

    def finish(dx):
        osend[dx, :HD, :] = acc[dx].astype(BF16)
        side = jnp.zeros((16, COLS), F32)
        for i, part in enumerate(thirds(mx[dx]) + thirds(ls[dx])):
            side = jnp.where(line == i, part, side)
        osend[dx, HD:, :] = side.astype(BF16)

    def o_copy(dx):
        h = lax.rem(x + dx, NX)
        return copy(osend.at[dx], orecv.at[dx], oss.at[dx], ors.at[dx], dev(h, y, z, c))

    def combine():
        held = [(osend if dx == 0 else orecv).at[dx] for dx in range(NX)]
        sides = [part[HD:, :].astype(F32) for part in held]
        tops = [side[0:1] + side[1:2] + side[2:3] for side in sides]
        counts = [side[3:4] + side[4:5] + side[5:6] for side in sides]
        top = jnp.maximum(jnp.maximum(tops[0], tops[1]), jnp.maximum(tops[2], tops[3]))
        shares = [jnp.exp2((t - top) * SCALE) for t in tops]
        inverse = 1.0 / sum(share * count for share, count in zip(shares, counts))
        total = sum((share * inverse) * part[:HD, :].astype(F32) for part, share in zip(held, shares))
        o_ref[...] = total.T.astype(BF16)

    def step(n, dx, at, n_next, dx_next, to):
        before, now = mp[dx], mx[dx]
        score(n_next, dx_next, to)
        weigh(n, dx, at, before, now)

    def q_wait(dx):
        q_copy(NX - dx).wait_recv()

    score(0, 0, s0)
    q_wait(1)
    step(0, 0, s0, 0, 1, s1)
    q_wait(3)
    step(0, 1, s1, 0, 3, s2)
    stage_opp(1)
    stage_opp(2)
    stage_y(1)
    stage_y(2)
    q_wait(2)
    step(0, 3, s2, 0, 2, s3)
    stage_own(5)
    stage_own(6)
    stage_c(1)
    step(0, 2, s3, 1, 0, s0)
    step(1, 0, s0, 1, 1, s1)
    step(1, 1, s1, 1, 3, s2)
    stage_opp(3)
    stage_opp(4)
    stage_y(3)
    stage_y(4)
    step(1, 3, s2, 1, 2, s3)
    stage_c(2)
    step(1, 2, s3, 2, 2, s0)

    def unit(n, carry):
        step(n, 2, s0, n, 1, s1)

        @pl.when(n == 2)
        def _():
            stage_own(7)

        @pl.when((n == 3) | (n == 4))
        def _():
            stage_opp(n + 2)
            stage_y(n + 2)

        step(n, 1, s1, n, 3, s2)

        @pl.when(n == 5)
        def _():
            stage_opp(7)
            stage_y(7)

        stage_c(n + 1)
        step(n, 3, s2, n + 1, 2, s0)
        return carry

    lax.fori_loop(2, 6, unit, 0)

    tail = [(n, dx) for dx in WAYS for n in (6, 7)] + [(n, 0) for n in range(2, NZ)]
    at, to = s0, s1
    for i, (n, dx) in enumerate(tail):
        if i == 0:
            stage_c(7)
        if i + 1 < len(tail):
            step(n, dx, at, *tail[i + 1], to)
            at, to = to, at
        else:
            weigh(n, dx, at, mp[dx], mx[dx])
        if n == NZ - 1:
            finish(dx)
            if dx:
                o_copy(dx).start()
    for dx in WAYS:
        o_copy(dx).wait_recv()
    combine()

    here = dev(x, y, z, 1 - c)
    one = kv.at[z, c, y]
    for n in range(NZ):
        if n != 5:
            copy(one, one, zs.at[0, n], rs.at[z, y], here).wait_send()
        if n != 6:
            copy(one, one, zs.at[1, n], rs.at[z, y], here).wait_send()
        for way in range(2):
            copy(one, one, ys.at[way, n], rs.at[z, y], here).wait_send()
        both_copy(n).wait_send()
    copy(one, one, yo.at[0], rs.at[z, y], here).wait_send()
    for dx in WAYS:
        q_copy(dx).wait_send()

    for dx in WAYS:
        o_copy(dx).wait_send()


def body(queries, keys, values):
    dma = pltpu.SemaphoreType.DMA
    scratch = [
        pltpu.VMEM(queries.shape, BF16),
        pltpu.VMEM((BLK, HD), BF16),
        pltpu.VMEM((BLK, HD), BF16),
        pltpu.VMEM((NZ, 2, NY, 2 * BLK, HD), BF16),
        pltpu.VMEM((NX, HD, COLS), BF16),
    ]
    scratch += [pltpu.VMEM((2 * BLK * NY, COLS), F32) for _ in range(4)]
    scratch += [pltpu.VMEM((NY, 1, COLS), F32) for _ in range(3)]
    scratch += [
        pltpu.VMEM((NX, HD, COLS), F32),
        pltpu.VMEM((NX, HD + 16, COLS), BF16),
        pltpu.VMEM((NX, HD + 16, COLS), BF16),
        dma((3,)), dma((NZ, NY)), dma((2, NZ)), dma((2, NZ)), dma((1,)), dma((NZ,)), dma((NZ,)),
        dma((NX,)), dma((NX,)), dma((NX,)), dma((NX,)),
    ]
    return pl.pallas_call(
        kernel,
        out_shape=jax.ShapeDtypeStruct(queries.shape, BF16),
        in_specs=[pl.BlockSpec(memory_space=pltpu.HBM)] * 3,
        out_specs=pl.BlockSpec(memory_space=pltpu.VMEM),
        scratch_shapes=scratch,
        compiler_params=pltpu.CompilerParams(
            collective_id=0, has_side_effects=True, vmem_limit_bytes=62 * 1024 * 1024
        ),
    )(queries, keys, values)


def solution(mesh):
    placed = (P("ctx", "head"), P("ctx", None), P("ctx", None))
    return jax.shard_map(
        body, mesh=mesh, in_specs=placed, out_specs=P("ctx", "head"), check_vma=False
    )
```

time: 60.3 us -> 49.2 us (0.82); the launches traced: 59.3 us -> 49.1 us
  Pallas kernels: 56 us -> 47.6 us
  local copies, waits for them, and re-layouts: 3.37 us -> 1.57 us
    pallas_call x1, Pallas kernels: 56 us -> 47.6 us  [body(): pl.pallas_call(kernel, out_shape=jax.ShapeDtypeStruct(queries.shape, BF16...]
    unnamed x7 -> x1, local copies, waits for them, and re-layouts: 3.37 us -> 1.57 us
where the time goes in v2:
time: 49.2 us; the launch traced here: 49.1 us
  Pallas kernels  47.6 us (97%)
  local copies, waits for them, and re-layouts  1.57 us (3%)
    pallas_call x1, Pallas kernels, body(): pl.pallas_call(kernel, out_shape=jax.ShapeDtypeStruct(queries.shape, BF16...  47.6 us
    unnamed x1, local copies, waits for them, and re-layouts  1.57 us

profile of v2, /device:TPU:1, one launch (start us, length us, event | category | flops | bytes accessed | tf_op | source)
XLA Modules:
  0.0 49.1 jit_solution(1074029651005729161)
XLA Ops:
  0.0 47.6 %shard_map.37 = bf16[512,128]{1,0:T(8,128)(2,1)} custom-call(bf16[512,128]{1,0:T(8,128)(2,1)} %q_hbm.1, bf16[512,128]{1,0:T(8,128)(2,1)} %k_hbm.1, bf16[512,128]{1,0:T(8,128)(2,1)} %v_hbm.1), custom_call_target="tpu_custom_call" | custom-call | tf_op jit(solution)/shard_map/pallas_call | solution.py:321
  47.6 1.6 %copy.5 = bf16[512,128]{1,0:T(8,128)(2,1)} copy(bf16[512,128]{1,0:T(8,128)(2,1)} %shard_map.37) | data formatting | bytes 262144

commit v3 on v2

--- a/solution.py
+++ b/solution.py
@@ -16,6 +16,9 @@
 EMPTY = -1e30
 HIDDEN = -2e30
 WAYS = (2, 1, 3)
+RING = {0: (1, 2), 1: (3,), 2: (4,), 3: (5,), 4: (6,)}
+OWN_WAY = {**RING, 6: (7,)}
+OPP_WAY = {**RING, 5: (7,)}
 F32 = jnp.float32
 BF16 = jnp.bfloat16
 
@@ -32,7 +35,6 @@
     y = lax.div(ctx, 2 * NZ)
     opp = lax.rem(y + 2, NY)
     yup, ydn = lax.rem(y + 1, NY), lax.rem(y + NY - 1, NY)
-    zup, zdn = lax.rem(z + 1, NZ), lax.rem(z + NZ - 1, NZ)
 
     def dev(xx, yy, zz, cc):
         return ((yy * NZ + zz) * 2 + cc, xx)
@@ -53,7 +55,7 @@
     barrier = pltpu.get_barrier_semaphore()
     targets = [dev(lax.rem(x + dx, NX), y, z, c) for dx in WAYS]
     targets += [dev(x, yy, z, c) for yy in (opp, yup, ydn)]
-    targets += [dev(x, y, zup, c), dev(x, y, zdn, c), dev(x, y, z, 1 - c)]
+    targets += [dev(x, y, lax.rem(z + d, NZ), c) for d in (1, NZ - 1)] + [dev(x, y, z, 1 - c)]
     for target in targets:
         pl.semaphore_signal(barrier, inc=1, device_id=target, device_id_type=MESH)
 
@@ -64,6 +66,13 @@
         mx[g] = jnp.full((1, COLS), EMPTY, F32)
         ls[g] = jnp.zeros((1, COLS), F32)
         acc[g] = jnp.zeros((HD, COLS), F32)
+    for yy in range(1, NY):
+
+        @pl.when(yy > y)
+        def _():
+            for zz in range(NZ):
+                kv[zz, c, yy] = jnp.zeros((2 * BLK, HD), BF16)
+
     loads[0].wait()
     qb[x] = turn(q_ref[...])
     loads[1].wait()
@@ -85,43 +94,53 @@
         part = kv.at[zz, c, yy]
         copy(part, part, yo.at[0], rs.at[zz, yy], dev(x, y, z, 1 - c)).wait_recv()
 
-    kv_send(z, y, yo.at[0], dev(x, opp, z, c))
-    kv_send(z, y, zs.at[0, 0], dev(x, y, zdn, c))
-    kv_send(z, y, zs.at[0, 7], dev(x, y, zup, c))
-    kv_send(z, y, ys.at[0, 0], dev(x, yup, z, c))
-    kv_send(z, y, ys.at[1, 0], dev(x, ydn, z, c))
+    def shift(n):
+        d, odd = (n + 1) // 2, n % 2
+        return d * (2 * odd - 1)
+
+    def place(n):
+        if not isinstance(n, int):
+            return lax.rem(z + NZ + lax.div(n + 1, 2) * (2 * lax.rem(n, 2) - 1), NZ)
+        return lax.rem(z + NZ + shift(n), NZ)
+
+    def kv_along(item, n):
+        zz = place(n)
+        for m in (OWN_WAY, OPP_WAY)[item].get(n, ()):
+            kv_send(zz, (y, opp)[item], zs.at[item, m], dev(x, y, lax.rem(zz + NZ - shift(m), NZ), c))
+
+    def send_y(n):
+        zz = place(n)
+
+        @pl.when(y < NY - 1)
+        def _():
+            kv_send(zz, y, ys.at[0, n], dev(x, yup, z, c))
+
+        @pl.when(y == 0)
+        def _():
+            kv_send(zz, y, ys.at[1, n], dev(x, ydn, z, c))
+
+    def stage_own(n):
+        zz = place(n)
+        kv_wait(zz, y)
+        kv_along(0, n)
+        send_y(n)
+
+    def stage_opp(n):
+        @pl.when(y >= 2)
+        def _():
+            kv_wait(place(n), opp)
+            kv_along(1, n)
+
+
+    @pl.when(y < 2)
+    def _():
+        kv_send(z, y, yo.at[0], dev(x, opp, z, c))
+
+    kv_along(0, 0)
+    send_y(0)
     for dx in (1, 3, 2):
         q_copy(dx).start()
 
-    def place(n):
-        d = lax.div(n + 1, 2) if not isinstance(n, int) else (n + 1) // 2
-        side = 2 * (n % 2 if isinstance(n, int) else lax.rem(n, 2)) - 1
-        return lax.rem(z + NZ + d * side, NZ)
-
-    def onward(n):
-        odd = n % 2 if isinstance(n, int) else lax.rem(n, 2)
-        return dev(x, y, odd * zdn + (1 - odd) * zup, c)
-
-    def stage_own(n):
-        zz = place(n)
-        kv_wait(zz, y)
-        if n in (1, 2, 3, 4, 6):
-            kv_send(zz, y, zs.at[0, n], onward(n))
-        kv_send(zz, y, ys.at[0, n], dev(x, yup, z, c))
-        kv_send(zz, y, ys.at[1, n], dev(x, ydn, z, c))
-
-    def stage_opp(n):
-        zz = place(n)
-        kv_wait(zz, opp)
-        if isinstance(n, int):
-            if n <= 5:
-                kv_send(zz, opp, zs.at[1, n], onward(n))
-        else:
-
-            @pl.when(n <= 5)
-            def _():
-                kv_send(zz, opp, zs.at[1, n], onward(n))
-
     def both_copy(n):
         zz = place(n)
         part = kv.at[zz, c]
@@ -129,8 +148,15 @@
 
     def stage_y(n):
         zz = place(n)
-        kv_wait(zz, yup)
-        kv_wait(zz, ydn)
+
+        @pl.when(y == NY - 1)
+        def _():
+            kv_wait(zz, yup)
+
+        @pl.when(y > 0)
+        def _():
+            kv_wait(zz, ydn)
+
         both_copy(n).start()
 
     def stage_c(n):
@@ -140,12 +166,8 @@
 
     stage_own(1)
     stage_own(2)
-    kv_wait(z, opp)
-    kv_send(z, opp, zs.at[1, 0], dev(x, y, zdn, c))
-    kv_send(z, opp, zs.at[1, 7], dev(x, y, zup, c))
+    stage_opp(0)
     stage_y(0)
-    stage_own(3)
-    stage_own(4)
     stage_c(0)
 
     apart = lax.broadcasted_iota(jnp.int32, (BLK, COLS), 0) - lax.broadcasted_iota(jnp.int32, (BLK, COLS), 1)
@@ -217,6 +239,8 @@
     score(0, 0, s0)
     q_wait(1)
     step(0, 0, s0, 0, 1, s1)
+    stage_own(3)
+    stage_own(4)
     q_wait(3)
     step(0, 1, s1, 0, 3, s2)
     stage_opp(1)
@@ -225,10 +249,10 @@
     stage_y(2)
     q_wait(2)
     step(0, 3, s2, 0, 2, s3)
+    stage_c(1)
+    step(0, 2, s3, 1, 0, s0)
     stage_own(5)
     stage_own(6)
-    stage_c(1)
-    step(0, 2, s3, 1, 0, s0)
     step(1, 0, s0, 1, 1, s1)
     step(1, 1, s1, 1, 3, s2)
     stage_opp(3)
@@ -246,10 +270,12 @@
         def _():
             stage_own(7)
 
-        @pl.when((n == 3) | (n == 4))
-        def _():
-            stage_opp(n + 2)
-            stage_y(n + 2)
+        for m in (5, 6):
+
+            @pl.when(n == m - 2)
+            def _():
+                stage_opp(m)
+                stage_y(m)
 
         step(n, 1, s1, n, 3, s2)
 
@@ -278,23 +304,42 @@
             finish(dx)
             if dx:
                 o_copy(dx).start()
+    here = dev(x, y, z, 1 - c)
+    one = kv.at[z, c, y]
+
+    def sent(send):
+        copy(one, one, send, rs.at[z, y], here).wait_send()
+
+    for n in range(1, NZ):
+        sent(zs.at[0, n])
+    for n in range(NZ):
+        both_copy(n).wait_send()
+
+    @pl.when(y >= 2)
+    def _():
+        for n in range(1, NZ):
+            sent(zs.at[1, n])
+
+    @pl.when(y < 2)
+    def _():
+        sent(yo.at[0])
+
+    @pl.when(y < NY - 1)
+    def _():
+        for n in range(NZ):
+            sent(ys.at[0, n])
+
+    @pl.when(y == 0)
+    def _():
+        for n in range(NZ):
+            sent(ys.at[1, n])
+
+    for dx in WAYS:
+        q_copy(dx).wait_send()
+
     for dx in WAYS:
         o_copy(dx).wait_recv()
     combine()
-
-    here = dev(x, y, z, 1 - c)
-    one = kv.at[z, c, y]
-    for n in range(NZ):
-        if n != 5:
-            copy(one, one, zs.at[0, n], rs.at[z, y], here).wait_send()
-        if n != 6:
-            copy(one, one, zs.at[1, n], rs.at[z, y], here).wait_send()
-        for way in range(2):
-            copy(one, one, ys.at[way, n], rs.at[z, y], here).wait_send()
-        both_copy(n).wait_send()
-    copy(one, one, yo.at[0], rs.at[z, y], here).wait_send()
-    for dx in WAYS:
-        q_copy(dx).wait_send()
 
     for dx in WAYS:
         o_copy(dx).wait_send()

time: 49.2 us -> 47.8 us (0.972)
  Pallas kernels: 47.6 us -> 46.2 us
    pallas_call x1, Pallas kernels: 47.6 us -> 46.2 us  [body(): pl.pallas_call(kernel, out_shape=jax.ShapeDtypeStruct(queries.shape, BF16...]
where the time goes in v3:
time: 47.8 us; the launch traced here: 47.7 us
  Pallas kernels  46.2 us (97%)
  local copies, waits for them, and re-layouts  1.57 us (3%)
    pallas_call x1, Pallas kernels, body(): pl.pallas_call(kernel, out_shape=jax.ShapeDtypeStruct(queries.shape, BF16...  46.2 us
    unnamed x1, local copies, waits for them, and re-layouts  1.57 us

profile of v3, /device:TPU:1, one launch (start us, length us, event | category | flops | bytes accessed | tf_op | source)
XLA Modules:
  0.0 47.7 jit_solution(15214889466322549682)
XLA Ops:
  0.0 46.2 %shard_map.37 = bf16[512,128]{1,0:T(8,128)(2,1)} custom-call(bf16[512,128]{1,0:T(8,128)(2,1)} %q_hbm.1, bf16[512,128]{1,0:T(8,128)(2,1)} %k_hbm.1, bf16[512,128]{1,0:T(8,128)(2,1)} %v_hbm.1), custom_call_target="tpu_custom_call" | custom-call | tf_op jit(solution)/shard_map/pallas_call | solution.py:366
  46.2 1.6 %copy.5 = bf16[512,128]{1,0:T(8,128)(2,1)} copy(bf16[512,128]{1,0:T(8,128)(2,1)} %shard_map.37) | data formatting | bytes 262144

commit v4 on v3

--- a/solution.py
+++ b/solution.py
@@ -179,22 +179,30 @@
         zz, h = place(n), lax.rem(x + dx, NX)
         k = jnp.concatenate([kv[zz, :, slab(back), :BLK, :].reshape(2 * BLK, HD) for back in range(NY)], axis=0)
         s = jnp.dot(k, qb[h], preferred_element_type=F32)
-        parts = []
+        own = []
         for cc in range(2):
             ahead = (zz - z) * 1024 + (cc - c) * 512 + x * BLK
-            parts.append(jnp.where(apart <= -ahead, s[cc * BLK:(cc + 1) * BLK], HIDDEN))
-        for back in range(1, NY):
-            parts.append(jnp.where(back <= y, s[2 * back * BLK:2 * (back + 1) * BLK], HIDDEN))
-        s = jnp.concatenate(parts, axis=0)
-        to[...] = s
+            own.append(jnp.where(apart <= -ahead, s[cc * BLK:(cc + 1) * BLK], HIDDEN))
+        own = jnp.concatenate(own, axis=0)
+        to[:2 * BLK] = own
+        to[2 * BLK:] = s[2 * BLK:]
         before = mx[dx]
         mp[dx] = before
-        mx[dx] = jnp.maximum(before, jnp.max(s, axis=0, keepdims=True))
+        top = jnp.maximum(before, jnp.max(own, axis=0, keepdims=True))
+        for back in range(1, NY):
+            one = jnp.max(s[2 * back * BLK:2 * (back + 1) * BLK], axis=0, keepdims=True)
+            top = jnp.maximum(top, jnp.where(back <= y, one, HIDDEN))
+        mx[dx] = top
 
     def weigh(n, dx, at, before, now):
         zz = place(n)
         old = jnp.exp2((before - now) * SCALE)
-        p = jnp.exp2(at[...] * SCALE - now * SCALE)
+        now = now * SCALE
+        parts = []
+        for back in range(NY):
+            row = jnp.where(back <= y, now, -HIDDEN) if back else now
+            parts.append(jnp.exp2(at[2 * back * BLK:2 * (back + 1) * BLK] * SCALE - row))
+        p = jnp.concatenate(parts, axis=0)
         v = jnp.concatenate([kv[zz, cc, slab(back), BLK:, :] for back in range(NY) for cc in range(2)], axis=1)
         ls[dx] = ls[dx] * old + jnp.sum(p, axis=0, keepdims=True)
         acc[dx] = acc[dx] * old + jnp.dot(v, p.astype(BF16), preferred_element_type=F32)
@@ -270,16 +278,15 @@
         def _():
             stage_own(7)
 
-        for m in (5, 6):
-
-            @pl.when(n == m - 2)
-            def _():
+        @pl.when(n == 3)
+        def _():
+            for m in (5, 6):
                 stage_opp(m)
                 stage_y(m)
 
         step(n, 1, s1, n, 3, s2)
 
-        @pl.when(n == 5)
+        @pl.when(n == 4)
         def _():
             stage_opp(7)
             stage_y(7)

time: 47.8 us -> 45.4 us (0.950)
  Pallas kernels: 46.2 us -> 43.7 us
    pallas_call x1, Pallas kernels: 46.2 us -> 43.7 us  [body(): pl.pallas_call(kernel, out_shape=jax.ShapeDtypeStruct(queries.shape, BF16...]
where the time goes in v4:
time: 45.4 us; the launch traced here: 45.3 us
  Pallas kernels  43.7 us (96%)
  local copies, waits for them, and re-layouts  1.57 us (3%)
    pallas_call x1, Pallas kernels, body(): pl.pallas_call(kernel, out_shape=jax.ShapeDtypeStruct(queries.shape, BF16...  43.7 us
    unnamed x1, local copies, waits for them, and re-layouts  1.57 us

profile of v4, /device:TPU:1, one launch (start us, length us, event | category | flops | bytes accessed | tf_op | source)
XLA Modules:
  0.0 45.3 jit_solution(17674810195921509173)
XLA Ops:
  0.0 43.7 %shard_map.37 = bf16[512,128]{1,0:T(8,128)(2,1)} custom-call(bf16[512,128]{1,0:T(8,128)(2,1)} %q_hbm.1, bf16[512,128]{1,0:T(8,128)(2,1)} %k_hbm.1, bf16[512,128]{1,0:T(8,128)(2,1)} %v_hbm.1), custom_call_target="tpu_custom_call" | custom-call | tf_op jit(solution)/shard_map/pallas_call | solution.py:373
  43.8 1.6 %copy.5 = bf16[512,128]{1,0:T(8,128)(2,1)} copy(bf16[512,128]{1,0:T(8,128)(2,1)} %shard_map.37) | data formatting | bytes 262144

commit v5 on v4

--- a/solution.py
+++ b/solution.py
@@ -50,7 +50,7 @@
         pltpu.make_async_copy(k_hbm.at[rows], k_ref, ins.at[1]),
         pltpu.make_async_copy(v_hbm.at[rows], v_ref, ins.at[2]),
     ]
-    for load in loads:
+    for load in loads[::-1]:
         load.start()
     barrier = pltpu.get_barrier_semaphore()
     targets = [dev(lax.rem(x + dx, NX), y, z, c) for dx in WAYS]
@@ -62,6 +62,73 @@
     def turn(a):
         return a.astype(F32).T.astype(BF16)
 
+    loads[1].wait()
+    kv[z, c, y, :BLK, :] = k_ref[...]
+    loads[2].wait()
+    kv[z, c, y, BLK:, :] = turn(v_ref[...])
+
+    pl.semaphore_wait(barrier, len(targets))
+
+    def q_copy(dx):
+        part = qb.at[x]
+        return copy(part, part, qss.at[dx], qrs.at[dx], dev(lax.rem(x + dx, NX), y, z, c))
+
+    def kv_send(zz, yy, send, device):
+        part = kv.at[zz, c, yy]
+        copy(part, part, send, rs.at[zz, yy], device).start()
+
+    def kv_wait(zz, yy):
+        part = kv.at[zz, c, yy]
+        copy(part, part, yo.at[0], rs.at[zz, yy], dev(x, y, z, 1 - c)).wait_recv()
+
+    def shift(n):
+        d, odd = (n + 1) // 2, n % 2
+        return d * (2 * odd - 1)
+
+    def place(n):
+        if not isinstance(n, int):
+            return lax.rem(z + NZ + lax.div(n + 1, 2) * (2 * lax.rem(n, 2) - 1), NZ)
+        return lax.rem(z + NZ + shift(n), NZ)
+
+    def kv_along(item, n):
+        zz = place(n)
+        for m in (OWN_WAY, OPP_WAY)[item].get(n, ()):
+            kv_send(zz, (y, opp)[item], zs.at[item, m], dev(x, y, lax.rem(zz + NZ - shift(m), NZ), c))
+
+    def send_y(n):
+        zz = place(n)
+
+        @pl.when(y < NY - 1)
+        def _():
+            kv_send(zz, y, ys.at[0, n], dev(x, yup, z, c))
+
+        @pl.when(y == 0)
+        def _():
+            kv_send(zz, y, ys.at[1, n], dev(x, ydn, z, c))
+
+    def stage_own(n):
+        zz = place(n)
+        kv_wait(zz, y)
+        kv_along(0, n)
+        send_y(n)
+
+    def stage_opp(n):
+        @pl.when(y >= 2)
+        def _():
+            kv_wait(place(n), opp)
+            kv_along(1, n)
+
+
+    @pl.when(y < 2)
+    def _():
+        kv_send(z, y, yo.at[0], dev(x, opp, z, c))
+
+    kv_along(0, 0)
+    send_y(0)
+    loads[0].wait()
+    qb[x] = turn(q_ref[...])
+    for dx in (1, 3, 2):
+        q_copy(dx).start()
     for g in range(NY):
         mx[g] = jnp.full((1, COLS), EMPTY, F32)
         ls[g] = jnp.zeros((1, COLS), F32)
@@ -73,73 +140,6 @@
             for zz in range(NZ):
                 kv[zz, c, yy] = jnp.zeros((2 * BLK, HD), BF16)
 
-    loads[0].wait()
-    qb[x] = turn(q_ref[...])
-    loads[1].wait()
-    kv[z, c, y, :BLK, :] = k_ref[...]
-    loads[2].wait()
-    kv[z, c, y, BLK:, :] = turn(v_ref[...])
-
-    pl.semaphore_wait(barrier, len(targets))
-
-    def q_copy(dx):
-        part = qb.at[x]
-        return copy(part, part, qss.at[dx], qrs.at[dx], dev(lax.rem(x + dx, NX), y, z, c))
-
-    def kv_send(zz, yy, send, device):
-        part = kv.at[zz, c, yy]
-        copy(part, part, send, rs.at[zz, yy], device).start()
-
-    def kv_wait(zz, yy):
-        part = kv.at[zz, c, yy]
-        copy(part, part, yo.at[0], rs.at[zz, yy], dev(x, y, z, 1 - c)).wait_recv()
-
-    def shift(n):
-        d, odd = (n + 1) // 2, n % 2
-        return d * (2 * odd - 1)
-
-    def place(n):
-        if not isinstance(n, int):
-            return lax.rem(z + NZ + lax.div(n + 1, 2) * (2 * lax.rem(n, 2) - 1), NZ)
-        return lax.rem(z + NZ + shift(n), NZ)
-
-    def kv_along(item, n):
-        zz = place(n)
-        for m in (OWN_WAY, OPP_WAY)[item].get(n, ()):
-            kv_send(zz, (y, opp)[item], zs.at[item, m], dev(x, y, lax.rem(zz + NZ - shift(m), NZ), c))
-
-    def send_y(n):
-        zz = place(n)
-
-        @pl.when(y < NY - 1)
-        def _():
-            kv_send(zz, y, ys.at[0, n], dev(x, yup, z, c))
-
-        @pl.when(y == 0)
-        def _():
-            kv_send(zz, y, ys.at[1, n], dev(x, ydn, z, c))
-
-    def stage_own(n):
-        zz = place(n)
-        kv_wait(zz, y)
-        kv_along(0, n)
-        send_y(n)
-
-    def stage_opp(n):
-        @pl.when(y >= 2)
-        def _():
-            kv_wait(place(n), opp)
-            kv_along(1, n)
-
-
-    @pl.when(y < 2)
-    def _():
-        kv_send(z, y, yo.at[0], dev(x, opp, z, c))
-
-    kv_along(0, 0)
-    send_y(0)
-    for dx in (1, 3, 2):
-        q_copy(dx).start()
 
     def both_copy(n):
         zz = place(n)
@@ -258,20 +258,19 @@
     q_wait(2)
     step(0, 3, s2, 0, 2, s3)
     stage_c(1)
-    step(0, 2, s3, 1, 0, s0)
+    step(0, 2, s3, 1, 1, s0)
     stage_own(5)
     stage_own(6)
-    step(1, 0, s0, 1, 1, s1)
-    step(1, 1, s1, 1, 3, s2)
+    step(1, 1, s0, 1, 3, s1)
     stage_opp(3)
     stage_opp(4)
     stage_y(3)
     stage_y(4)
-    step(1, 3, s2, 1, 2, s3)
+    step(1, 3, s1, 1, 2, s2)
     stage_c(2)
-    step(1, 2, s3, 2, 2, s0)
-
-    def unit(n, carry):
+    step(1, 2, s2, 2, 2, s0)
+
+    def unit(n):
         step(n, 2, s0, n, 1, s1)
 
         @pl.when(n == 2)
@@ -293,11 +292,11 @@
 
         stage_c(n + 1)
         step(n, 3, s2, n + 1, 2, s0)
-        return carry
-
-    lax.fori_loop(2, 6, unit, 0)
-
-    tail = [(n, dx) for dx in WAYS for n in (6, 7)] + [(n, 0) for n in range(2, NZ)]
+
+    for n in range(2, 6):
+        unit(n)
+
+    tail = [(n, dx) for dx in WAYS for n in (6, 7)] + [(n, 0) for n in range(1, NZ)]
     at, to = s0, s1
     for i, (n, dx) in enumerate(tail):
         if i == 0:

time: 45.4 us -> 44.5 us (0.980)
  Pallas kernels: 43.7 us -> 42.9 us
    pallas_call x1, Pallas kernels: 43.7 us -> 42.9 us  [body(): pl.pallas_call(kernel, out_shape=jax.ShapeDtypeStruct(queries.shape, BF16...]
where the time goes in v5:
time: 44.5 us; the launch traced here: 44.4 us
  Pallas kernels  42.9 us (96%)
  local copies, waits for them, and re-layouts  1.57 us (4%)
    pallas_call x1, Pallas kernels, body(): pl.pallas_call(kernel, out_shape=jax.ShapeDtypeStruct(queries.shape, BF16...  42.9 us
    unnamed x1, local copies, waits for them, and re-layouts  1.57 us

profile of v5, /device:TPU:1, one launch (start us, length us, event | category | flops | bytes accessed | tf_op | source)
XLA Modules:
  0.0 44.4 jit_solution(4807095558376576714)
XLA Ops:
  0.0 42.9 %shard_map.37 = bf16[512,128]{1,0:T(8,128)(2,1)} custom-call(bf16[512,128]{1,0:T(8,128)(2,1)} %q_hbm.1, bf16[512,128]{1,0:T(8,128)(2,1)} %k_hbm.1, bf16[512,128]{1,0:T(8,128)(2,1)} %v_hbm.1), custom_call_target="tpu_custom_call" | custom-call | tf_op jit(solution)/shard_map/pallas_call | solution.py:372
  42.9 1.6 %copy.5 = bf16[512,128]{1,0:T(8,128)(2,1)} copy(bf16[512,128]{1,0:T(8,128)(2,1)} %shard_map.37) | data formatting | bytes 262144

commit v6 on v5

--- a/solution.py
+++ b/solution.py
@@ -179,16 +179,19 @@
         zz, h = place(n), lax.rem(x + dx, NX)
         k = jnp.concatenate([kv[zz, :, slab(back), :BLK, :].reshape(2 * BLK, HD) for back in range(NY)], axis=0)
         s = jnp.dot(k, qb[h], preferred_element_type=F32)
-        own = []
-        for cc in range(2):
-            ahead = (zz - z) * 1024 + (cc - c) * 512 + x * BLK
-            own.append(jnp.where(apart <= -ahead, s[cc * BLK:(cc + 1) * BLK], HIDDEN))
-        own = jnp.concatenate(own, axis=0)
+        own = s[:2 * BLK]
+        if n == 0:
+            parts = []
+            for cc in range(2):
+                ahead = (cc - c) * 512 + x * BLK
+                parts.append(jnp.where(apart <= -ahead, s[cc * BLK:(cc + 1) * BLK], HIDDEN))
+            own = jnp.concatenate(parts, axis=0)
         to[:2 * BLK] = own
         to[2 * BLK:] = s[2 * BLK:]
         before = mx[dx]
         mp[dx] = before
-        top = jnp.maximum(before, jnp.max(own, axis=0, keepdims=True))
+        one = jnp.max(own, axis=0, keepdims=True)
+        top = jnp.maximum(before, jnp.where(zz < z, one, HIDDEN) if n else one)
         for back in range(1, NY):
             one = jnp.max(s[2 * back * BLK:2 * (back + 1) * BLK], axis=0, keepdims=True)
             top = jnp.maximum(top, jnp.where(back <= y, one, HIDDEN))
@@ -200,7 +203,9 @@
         now = now * SCALE
         parts = []
         for back in range(NY):
-            row = jnp.where(back <= y, now, -HIDDEN) if back else now
+            row = now
+            if back or n:
+                row = jnp.where(back <= y if back else zz < z, now, -HIDDEN)
             parts.append(jnp.exp2(at[2 * back * BLK:2 * (back + 1) * BLK] * SCALE - row))
         p = jnp.concatenate(parts, axis=0)
         v = jnp.concatenate([kv[zz, cc, slab(back), BLK:, :] for back in range(NY) for cc in range(2)], axis=1)

time: 44.5 us -> 44.5 us (level)
  no operation moved by 1% of the time
where the time goes in v6:
time: 44.5 us; the launch traced here: 44.4 us
  Pallas kernels  42.8 us (96%)
  local copies, waits for them, and re-layouts  1.57 us (4%)
    pallas_call x1, Pallas kernels, body(): pl.pallas_call(kernel, out_shape=jax.ShapeDtypeStruct(queries.shape, BF16...  42.8 us
    unnamed x1, local copies, waits for them, and re-layouts  1.57 us

profile of v6, /device:TPU:1, one launch (start us, length us, event | category | flops | bytes accessed | tf_op | source)
XLA Modules:
  0.0 44.4 jit_solution(15961622827878476326)
XLA Ops:
  0.0 42.8 %shard_map.37 = bf16[512,128]{1,0:T(8,128)(2,1)} custom-call(bf16[512,128]{1,0:T(8,128)(2,1)} %q_hbm.1, bf16[512,128]{1,0:T(8,128)(2,1)} %k_hbm.1, bf16[512,128]{1,0:T(8,128)(2,1)} %v_hbm.1), custom_call_target="tpu_custom_call" | custom-call | tf_op jit(solution)/shard_map/pallas_call | solution.py:377
  42.8 1.6 %copy.5 = bf16[512,128]{1,0:T(8,128)(2,1)} copy(bf16[512,128]{1,0:T(8,128)(2,1)} %shard_map.37) | data formatting | bytes 262144
